TPU v7x, 256 devices: a whole 4x4x8 slice. The times are simulated.
256 devices in a mesh: own: 8 (over z), col: 8 (over x, core), mlp: 4 (over y).
Axes of the slice: x: 4, y: 4, z: 8, core: 2. Of those that a mesh axis runs over, the one named last changes fastest.
Arguments:
- features: bfloat16 [262144, 512], P(('own', 'col')), may hold values from -6 to 6
- nbr_page: int32 [8192, 32], P(('own', 'col')), may hold values from 0 to 262143, as said below
- nbr_weight: bfloat16 [8192, 32], P(('own', 'col')), may hold values from 0.0049743652 to 0.29882812
- labels: int32 [8192], P(('own', 'col')), may hold values from 0 to 255
- w_one: bfloat16 [512, 2048], P(None, 'mlp'), may hold values from -0.25 to 0.25
- w_two: bfloat16 [2048, 256], P('mlp'), may hold values from -0.125 to 0.125
Outputs:
- grad_one: float32 [512, 2048], P(None, 'mlp')
- grad_two: float32 [2048, 256], P('mlp')
Inputs may be any that keep to these rules, and one draw needn't show every extreme that they name: `nbr_page`: page p is held by owner p // 4096 (owners numbered along own then col) at its row p % 4096. The 32 neighbours of a target are distinct pages listed in non-decreasing order of owner. Of the 4096 neighbour entries of the targets of one index of own and col, at most 128 fall on one owner; one owner receives exactly 128 entries from every index, and some owners receive none from some indices.
All inputs are finite; a program needn't handle non-finite values.
Results may differ from a plain program's by a relative error of at most 0.011.
Values may be sent and summed in bfloat16 or wider, within the bound.
No kernel may reach another device: no remote copies, remote signals or barrier semaphores. Data moves between devices by JAX's collectives and lax.ppermute only.
A program may use at most 128 MiB of HBM per device.

v0:
```python
import jax
import jax.numpy as jnp
from jax import lax
from jax.sharding import PartitionSpec as P


def body(features, nbr_page, nbr_weight, labels, w_one, w_two):
    rows_dev = features.shape[0]
    width_f = features.shape[1]
    targets = nbr_page.shape[0]
    width_k = nbr_page.shape[1]
    owners = lax.axis_size(("own", "col"))
    entries = targets * width_k
    capacity = 2 * entries // owners
    owner_ids = nbr_page // rows_dev
    local_row = nbr_page % rows_dev
    owner_range = jnp.arange(owners, dtype=jnp.int32)
    matches = (owner_ids[:, :, None] == owner_range[None, None, :]).astype(jnp.int32)
    row_count = jnp.sum(matches, axis=1)
    earlier_rows = jnp.cumsum(row_count, axis=0) - row_count
    before_owner = jnp.cumsum(row_count, axis=1) - row_count
    first_slot = earlier_rows - before_owner + owner_range[None, :] * capacity
    slot_ids = (
        jnp.sum(matches * first_slot[:, None, :], axis=2)
        + jnp.arange(width_k, dtype=jnp.int32)[None, :]
    )
    flat_slot = slot_ids.reshape(-1)
    requests = jnp.zeros((owners * capacity,), jnp.int32).at[flat_slot].set(local_row.reshape(-1))
    requests = requests.reshape(owners, capacity)
    asked_rows = lax.all_to_all(requests, ("own", "col"), split_axis=0, concat_axis=0, tiled=True)
    fetched = features[asked_rows]
    returned = lax.all_to_all(fetched, ("own", "col"), split_axis=0, concat_axis=0, tiled=True)
    received = returned.reshape(owners * capacity, width_f)
    contract_first = (((0,), (0,)), ((), ()))
    target_ids = jnp.broadcast_to(
        jnp.arange(targets, dtype=jnp.int32)[:, None], (targets, width_k)
    ).reshape(-1)
    spread = (
        jnp.zeros((targets, owners * capacity), jnp.bfloat16)
        .at[target_ids, flat_slot]
        .set(nbr_weight.reshape(-1))
    )
    pre_act = jnp.dot(received, w_one, preferred_element_type=jnp.float32)
    active = jnp.maximum(pre_act, 0.0).astype(jnp.bfloat16)
    hidden = jnp.dot(spread, active, preferred_element_type=jnp.float32).astype(jnp.bfloat16)
    partial_logits = jnp.dot(hidden, w_two, preferred_element_type=jnp.float32)
    logits = lax.psum(partial_logits, "mlp")
    exponent = jnp.exp(logits)
    probability = exponent / jnp.sum(exponent, axis=1, keepdims=True)
    classes = w_two.shape[1]
    onehot_label = (labels[:, None] == jnp.arange(classes, dtype=jnp.int32)[None, :]).astype(
        jnp.float32
    )
    d_logits = (probability - onehot_label).astype(jnp.bfloat16)
    grad_two = lax.dot_general(hidden, d_logits, contract_first, preferred_element_type=jnp.float32)
    d_hidden = lax.dot_general(
        d_logits, w_two, (((1,), (1,)), ((), ())), preferred_element_type=jnp.float32
    ).astype(jnp.bfloat16)
    positive = (pre_act > 0).astype(jnp.float32)
    scattered = lax.dot_general(
        spread, d_hidden, contract_first, preferred_element_type=jnp.float32
    )
    d_pre = (scattered * positive).astype(jnp.bfloat16)
    grad_one = lax.dot_general(received, d_pre, contract_first, preferred_element_type=jnp.float32)
    grad_one, grad_two = lax.psum((grad_one, grad_two), ("own", "col"))
    return (grad_one, grad_two)


def solution(mesh):
    placed = (
        P(("own", "col"), None),
        P(("own", "col"), None),
        P(("own", "col"), None),
        P(("own", "col")),
        P(None, "mlp"),
        P("mlp", None),
    )
    return jax.shard_map(
        body,
        mesh=mesh,
        in_specs=placed,
        out_specs=(P(None, "mlp"), P("mlp", None)),
        check_vma=False,
    )
```

profile of v0, /device:TPU:8, one launch (start us, length us, event | category | flops | bytes accessed | tf_op | source)
XLA Modules:
  0.0 551.1 jit_solution(711926448814235918)
XLA Ops:
  7.2 0.8 add_select_fusion
  8.6 0.2 reduce_window_sum.22
  8.8 0.2 select_reduce_fusion
  9.4 15.5 %scatter_custom_fusion = s32[8192]{0:T(1024)S(1)} fusion(s32[4096]{0:T(1024)S(1)} %bitcast.22, s32[4096]{0:T(1024)S(1)} %reshape.163, s32[]{:T(128)} %constant.41.clone.1), kind=kCustom, calls=%fused_computation.34 | custom fusion | bytes 32772 | tf_op jit(solution)/shard_map/scatter | solution.py:28
  25.0 21.3 %all_to_all.17 = s32[64,1,128]{2,1,0:T(1,128)S(1)} all-to-all(s32[64,1,128]{2,1,0:T(1,128)S(1)} %bitcast.23), channel_id=1, replica_groups=mesh['own'=8,'col'=8,'mlp'=4] {'own','col'}, dimensions={0} | all-to-all | bytes 65536 | tf_op jit(solution)/shard_map/all_to_all | solution.py:30
  46.3 36.5 %gather_fusion = bf16[8192,512]{1,0:T(8,128)(2,1)} fusion(bf16[4096,512]{1,0:T(8,128)(2,1)} %param.6, s32[8192]{0:T(1024)S(1)} %fusion.7), kind=kCustom, calls=%fused_computation | custom fusion | bytes 16809984 | tf_op jit(solution)/shard_map/gather | solution.py:31
  82.8 5.9 %all-to-all-start.1 = ((bf16[64,128,512]{2,1,0:T(8,128)(2,1)}), bf16[64,128,512]{2,1,0:T(8,128)(2,1)}, u32[]{:S(2)}, u32[]{:S(2)}) async-start(bf16[64,128,512]{2,1,0:T(8,128)(2,1)} %bitcast.21), calls=%async_computation.1 | async-start | bytes 16777216 | tf_op jit(solution)/shard_map/all_to_all | solution.py:32
  88.8 0.1 copy.23
  89.1 0.1 and_reduce_fusion
  89.3 30.4 %scatter_custom_fusion.1 = bf16[1048576]{0:T(1024)(128)(2,1)} fusion(s32[4096]{0:T(1024)S(1)} %broadcast_select_fusion, bf16[4096]{0:T(1024)(128)(2,1)S(1)} %reshape.169, bf16[]{:T(256)} %constant.50.clone.1), kind=kCustom, calls=%fused_computation.10 | custom fusion | bytes 2097154
  119.7 2.8 reshape.150
  122.5 152.3 %all-to-all-done.1 = bf16[64,128,512]{2,1,0:T(8,128)(2,1)} async-done(((bf16[64,128,512]{2,1,0:T(8,128)(2,1)}), bf16[64,128,512]{2,1,0:T(8,128)(2,1)}, u32[]{:S(2)}, u32[]{:S(2)}) %all-to-all-start.1) | async-done | bytes 8388640 | tf_op jit(solution)/shard_map/all_to_all | solution.py:32
  274.8 7.1 %fusion.15 = f32[8192,512]{1,0:T(8,128)S(1)} fusion(bf16[8192,512]{1,0:T(8,128)(2,1)} %bitcast.5, bf16[512,512]{1,0:T(8,128)(2,1)S(1)} %copy-done), kind=kOutput, calls=%fused_computation.43 | convolution fusion | flops 4294967296 | bytes 25690112 | tf_op jit(solution)/shard_map/dot_general | solution.py:43
  281.9 1.6 fusion.3
  283.5 4.1 copy-done.1
  287.6 0.8 fusion.16
  288.5 42.6 %all-reduce.4.cloned.1.call-done = f32[128,256]{1,0:T(8,128)} async-done(((f32[128,256]{1,0:T(8,128)}), f32[128,256]{1,0:T(8,128)}) %all-reduce.4.cloned.1.call-update) | async-done | bytes 131088 | tf_op jit(solution)/shard_map/psum | solution.py:47
  331.1 1.0 exponential_reduce_fusion
  332.1 1.1 convolution_convert_fusion
  333.2 16.1 %fusion.2 = f32[512,512]{1,0:T(8,128)} fusion(bf16[8192,512]{1,0:T(8,128)(2,1)} %bitcast.5, f32[8192,512]{1,0:T(8,128)} %copy-done.1, bf16[128,8192]{1,0:T(8,128)(2,1)S(1)} %reshape.150, bf16[128,512]{1,0:T(8,128)(2,1)S(1)} %convolution_convert_fusion), kind=kOutput, calls=%fused_computation.7 | convolution fusion | flops 5381292032 | bytes 28442624 | tf_op jit(solution)/shard_map/dot_general | solution.py:64
  349.3 1.1 fusion.14
  350.5 189.7 %all-reduce.6.cloned.1.call-done = (f32[512,512]{1,0:T(8,128)}, f32[512,256]{1,0:T(8,128)}) async-done(((f32[512,512]{1,0:T(8,128)}, f32[512,256]{1,0:T(8,128)}), (f32[512,512]{1,0:T(8,128)}, f32[512,256]{1,0:T(8,128)})) %all-reduce.6.cloned.1.call-update) | async-done | bytes 1572880 | tf_op jit(solution)/shard_map/psum | solution.py:65
  540.2 2.3 copy.27
  542.4 1.9 copy.28
  (38 shorter events, 1.4 us)
Async XLA Ops:
  7.2 267.6 %copy-start = (bf16[512,512]{1,0:T(8,128)(2,1)S(1)}, bf16[512,512]{1,0:T(8,128)(2,1)}, u32[]{:S(2)}) copy-start(bf16[512,512]{1,0:T(8,128)(2,1)} %param.10) | copy-start | bytes 1572868
  82.8 6.0 %copy-start.4 = (bf16[128,32]{0,1:T(8,128)(2,1)S(1)}, bf16[128,32]{0,1:T(8,128)(2,1)}, u32[]{:S(2)}) copy-start(bf16[128,32]{0,1:T(8,128)(2,1)} %param.8) | copy-start | bytes 24580
  82.8 6.2 %copy-start.7 = (s32[2]{0:T(128)S(1)}, s32[2]{0:T(128)}, u32[]{:S(2)}) copy-start(s32[2]{0:T(128)} %constant.51) | copy-start | bytes 28
  82.8 6.3 %copy-start.6 = (s32[2]{0:T(128)S(1)}, s32[2]{0:T(128)}, u32[]{:S(2)}) copy-start(s32[2]{0:T(128)} %constant.54) | copy-start | bytes 28
  82.8 191.9 %all-to-all-start.1 = ((bf16[64,128,512]{2,1,0:T(8,128)(2,1)}), bf16[64,128,512]{2,1,0:T(8,128)(2,1)}, u32[]{:S(2)}, u32[]{:S(2)}) async-start(bf16[64,128,512]{2,1,0:T(8,128)(2,1)} %bitcast.21), calls=%async_computation.1 | async-start | bytes 16777216 | tf_op jit(solution)/shard_map/all_to_all | solution.py:32
  88.7 242.3 %all-reduce.4.cloned.1.call-start = ((), (), s32[]{:S(2)}) async-start(), calls=%async_computation.2 | async-start | bytes 262144 | tf_op jit(solution)/shard_map/psum | solution.py:47
  281.9 5.7 %copy-start.1 = (f32[8192,512]{1,0:T(8,128)}, f32[8192,512]{1,0:T(8,128)S(1)}, u32[]{:S(2)}) copy-start(f32[8192,512]{1,0:T(8,128)S(1)} %fusion.15) | copy-start | bytes 50331652
  281.9 5.7 %copy-start.3 = (bf16[512,256]{1,0:T(8,128)(2,1)S(1)}, bf16[512,256]{1,0:T(8,128)(2,1)}, u32[]{:S(2)}) copy-start(bf16[512,256]{1,0:T(8,128)(2,1)} %param.11) | copy-start | bytes 786436
  281.9 50.2 %copy-start.5 = (s32[128]{0:T(128)S(1)}, s32[128]{0:T(128)}, u32[]{:S(2)}) copy-start(s32[128]{0:T(128)} %param.9) | copy-start | bytes 1540
  288.5 251.7 %all-reduce.6.cloned.1.call-start = ((), (), s32[]{:S(2)}) async-start(), calls=%async_computation.3 | async-start | bytes 3145728 | tf_op jit(solution)/shard_map/psum | solution.py:65
  333.2 16.1 %copy-start.2 = (f32[128,256]{1,0:T(8,128)S(1)}, f32[128,256]{1,0:T(8,128)}, u32[]{:S(2)}) copy-start(f32[128,256]{1,0:T(8,128)} %all-reduce.4.cloned.1.call-done) | copy-start | bytes 393220
Sparse Core Ops, SparseCore 0:
  288.6 42.4 all-reduce.3
  350.6 189.5 all-reduce.5
where the time goes:
time: 552 us; the launch traced here: 551 us
  waiting for transfers between devices  385 us (70%)
  local copies, waits for them, and re-layouts  94.5 us (17%)
  matrix products  27.8 us (5%)
  blocking collectives  21.3 us (4%)
  between operations  14.3 us (3%)
  starting transfers between devices  5.97 us (1%)
    psum x1, waiting for transfers between devices, body(): grad_one, grad_two = lax.psum((grad_one, grad_two), ('own', 'col'))  190 us
    all_to_all x1, waiting for transfers between devices, body(): lax.all_to_all(fetched, ('own', 'col'), split_axis=0, concat_axis=0, tile...  152 us
    psum x1, waiting for transfers between devices, body(): logits = lax.psum(partial_logits, 'mlp')  42.6 us
    unnamed x20, local copies, waits for them, and re-layouts  38.8 us
    gather x1, local copies, waits for them, and re-layouts, body(): fetched = features[asked_rows]  36.5 us
    all_to_all x1, blocking collectives, body(): lax.all_to_all(requests, ('own', 'col'), split_axis=0, concat_axis=0, til...  21.3 us
    dot_general x1, matrix products, body(): lax.dot_general(received, d_pre, contract_first, preferred_element_type=j...  16.1 us
    scatter x1, local copies, waits for them, and re-layouts, body(): jnp.zeros((owners * capacity,), jnp.int32).at[flat_slot]  15.5 us
  transfers between devices with their start and end apart: 3, of which 3 were waited for; matrix products, arithmetic and copies ran while one was open for 6% of the time, Pallas kernels for 0%

commit v1 on v0

--- a/solution.py
+++ b/solution.py
@@ -2,6 +2,7 @@
 import jax.numpy as jnp
 from jax import lax
 from jax.sharding import PartitionSpec as P
+from jax.lax import all_gather
 
 
 def body(features, nbr_page, nbr_weight, labels, w_one, w_two):
@@ -44,7 +45,7 @@
     active = jnp.maximum(pre_act, 0.0).astype(jnp.bfloat16)
     hidden = jnp.dot(spread, active, preferred_element_type=jnp.float32).astype(jnp.bfloat16)
     partial_logits = jnp.dot(hidden, w_two, preferred_element_type=jnp.float32)
-    logits = lax.psum(partial_logits, "mlp")
+    logits = jnp.sum(all_gather(partial_logits, "mlp"), 0)
     exponent = jnp.exp(logits)
     probability = exponent / jnp.sum(exponent, axis=1, keepdims=True)
     classes = w_two.shape[1]

time: 552 us -> 517 us (0.937)
  waiting for transfers between devices: 385 us -> 338 us
  blocking collectives: 21.3 us -> 34.4 us
    psum x1 -> x0, waiting for transfers between devices: 42.6 us -> none  [body(): logits = lax.psum(partial_logits, 'mlp')]
    all_gather x0 -> x1, blocking collectives: none -> 13.1 us  [body(): logits = jnp.sum(all_gather(partial_logits, 'mlp'), 0)]
    unnamed x20 -> x18, local copies, waits for them, and re-layouts: 38.8 us -> 38.8 us
  transfers between devices with their start and end apart: 3 -> 2, of which waited for: 3 -> 2; matrix products, arithmetic and copies ran while one was open for 6% -> 7% of each run, Pallas kernels for 0% -> 0%
where the time goes in v1:
time: 517 us; the launch traced here: 516 us
  waiting for transfers between devices  338 us (65%)
  local copies, waits for them, and re-layouts  94.5 us (18%)
  blocking collectives  34.4 us (7%)
  matrix products  27.2 us (5%)
  between operations  14.3 us (3%)
  starting transfers between devices  5.93 us (1%)
    psum x1, waiting for transfers between devices, body(): grad_one, grad_two = lax.psum((grad_one, grad_two), ('own', 'col'))  186 us
    all_to_all x1, waiting for transfers between devices, body(): lax.all_to_all(fetched, ('own', 'col'), split_axis=0, concat_axis=0, tile...  152 us
    unnamed x18, local copies, waits for them, and re-layouts  38.8 us
    gather x1, local copies, waits for them, and re-layouts, body(): fetched = features[asked_rows]  36.5 us
    all_to_all x1, blocking collectives, body(): lax.all_to_all(requests, ('own', 'col'), split_axis=0, concat_axis=0, til...  21.3 us
    dot_general x1, matrix products, body(): lax.dot_general(received, d_pre, contract_first, preferred_element_type=j...  16.1 us
    scatter x1, local copies, waits for them, and re-layouts, body(): jnp.zeros((owners * capacity,), jnp.int32).at[flat_slot]  15.5 us
    all_gather x1, blocking collectives, body(): logits = jnp.sum(all_gather(partial_logits, 'mlp'), 0)  13.1 us
  transfers between devices with their start and end apart: 2, of which 2 were waited for; matrix products, arithmetic and copies ran while one was open for 7% of the time, Pallas kernels for 0%

profile of v1, /device:TPU:8, one launch (start us, length us, event | category | flops | bytes accessed | tf_op | source)
XLA Modules:
  0.0 516.3 jit_solution(13794221402228512433)
XLA Ops:
  7.2 0.8 add_select_fusion
  8.0 0.1 convert_reduce_fusion
  8.6 0.2 reduce_window_sum.22
  8.8 0.2 select_reduce_fusion
  9.4 15.5 %scatter_custom_fusion = s32[8192]{0:T(1024)S(1)} fusion(s32[4096]{0:T(1024)S(1)} %bitcast.24, s32[4096]{0:T(1024)S(1)} %reshape.163, s32[]{:T(128)} %constant.41.clone.1), kind=kCustom, calls=%fused_computation.34 | custom fusion | bytes 32772 | tf_op jit(solution)/shard_map/scatter | solution.py:29
  25.0 21.3 %all_to_all.17 = s32[64,1,128]{2,1,0:T(1,128)S(1)} all-to-all(s32[64,1,128]{2,1,0:T(1,128)S(1)} %bitcast.25), channel_id=1, replica_groups=mesh['own'=8,'col'=8,'mlp'=4] {'own','col'}, dimensions={0} | all-to-all | bytes 65536 | tf_op jit(solution)/shard_map/all_to_all | solution.py:31
  46.3 36.5 %gather_fusion = bf16[8192,512]{1,0:T(8,128)(2,1)} fusion(bf16[4096,512]{1,0:T(8,128)(2,1)} %param.6, s32[8192]{0:T(1024)S(1)} %fusion.7), kind=kCustom, calls=%fused_computation | custom fusion | bytes 16809984 | tf_op jit(solution)/shard_map/gather | solution.py:32
  82.8 5.9 %all-to-all-start.1 = ((bf16[64,128,512]{2,1,0:T(8,128)(2,1)}), bf16[64,128,512]{2,1,0:T(8,128)(2,1)}, u32[]{:S(2)}, u32[]{:S(2)}) async-start(bf16[64,128,512]{2,1,0:T(8,128)(2,1)} %bitcast.22), calls=%async_computation.1 | async-start | bytes 16777216 | tf_op jit(solution)/shard_map/all_to_all | solution.py:33
  88.8 0.1 copy.23
  89.1 0.1 and_reduce_fusion
  89.3 30.4 %scatter_custom_fusion.1 = bf16[1048576]{0:T(1024)(128)(2,1)} fusion(s32[4096]{0:T(1024)S(1)} %broadcast_select_fusion, bf16[4096]{0:T(1024)(128)(2,1)S(1)} %reshape.169, bf16[]{:T(256)} %constant.50.clone.1), kind=kCustom, calls=%fused_computation.10 | custom fusion | bytes 2097154
  119.7 2.8 reshape.150
  122.5 152.3 %all-to-all-done.1 = bf16[64,128,512]{2,1,0:T(8,128)(2,1)} async-done(((bf16[64,128,512]{2,1,0:T(8,128)(2,1)}), bf16[64,128,512]{2,1,0:T(8,128)(2,1)}, u32[]{:S(2)}, u32[]{:S(2)}) %all-to-all-start.1) | async-done | bytes 8388640 | tf_op jit(solution)/shard_map/all_to_all | solution.py:33
  274.8 7.1 %fusion.15 = f32[8192,512]{1,0:T(8,128)S(1)} fusion(bf16[8192,512]{1,0:T(8,128)(2,1)} %bitcast.5, bf16[512,512]{1,0:T(8,128)(2,1)S(1)} %copy-done), kind=kOutput, calls=%fused_computation.43 | convolution fusion | flops 4294967296 | bytes 25690112 | tf_op jit(solution)/shard_map/dot_general | solution.py:44
  281.9 1.6 fusion.3
  283.5 4.1 copy-done.1
  287.6 0.2 fusion.16
  287.8 13.1 %all-gather = f32[512,256]{1,0:T(8,128)S(1)} all-gather(f32[128,256]{1,0:T(8,128)S(1)} %fusion.16), channel_id=2, replica_groups=mesh['own'=8,'col'=8,'mlp'=4] {'mlp'}, dimensions={0}, use_global_device_ids=true | all-gather | bytes 655360 | tf_op jit(solution)/shard_map/all_gather | solution.py:48
  301.0 1.2 convolution_convert_fusion
  302.2 1.1 fusion.14
  303.3 16.1 %fusion.2 = f32[512,512]{1,0:T(8,128)} fusion(bf16[8192,512]{1,0:T(8,128)(2,1)} %bitcast.5, f32[8192,512]{1,0:T(8,128)} %copy-done.1, bf16[128,8192]{1,0:T(8,128)(2,1)S(1)} %reshape.150, bf16[128,512]{1,0:T(8,128)(2,1)S(1)} %convolution_convert_fusion), kind=kOutput, calls=%fused_computation.7 | convolution fusion | flops 5381292032 | bytes 28442624 | tf_op jit(solution)/shard_map/dot_general | solution.py:65
  319.4 185.9 %all-reduce.3.cloned.1.call-done = (f32[512,512]{1,0:T(8,128)}, f32[512,256]{1,0:T(8,128)}) async-done(((f32[512,512]{1,0:T(8,128)}, f32[512,256]{1,0:T(8,128)}), (f32[512,512]{1,0:T(8,128)}, f32[512,256]{1,0:T(8,128)})) %all-reduce.3.cloned.1.call-update) | async-done | bytes 1572880 | tf_op jit(solution)/shard_map/psum | solution.py:66
  505.3 2.3 copy.26
  507.6 1.9 copy.27
  (35 shorter events, 1.3 us)
Async XLA Ops:
  7.2 267.6 %copy-start = (bf16[512,512]{1,0:T(8,128)(2,1)S(1)}, bf16[512,512]{1,0:T(8,128)(2,1)}, u32[]{:S(2)}) copy-start(bf16[512,512]{1,0:T(8,128)(2,1)} %param.10) | copy-start | bytes 1572868
  82.8 6.0 %copy-start.3 = (bf16[128,32]{0,1:T(8,128)(2,1)S(1)}, bf16[128,32]{0,1:T(8,128)(2,1)}, u32[]{:S(2)}) copy-start(bf16[128,32]{0,1:T(8,128)(2,1)} %param.8) | copy-start | bytes 24580
  82.8 6.2 %copy-start.6 = (s32[2]{0:T(128)S(1)}, s32[2]{0:T(128)}, u32[]{:S(2)}) copy-start(s32[2]{0:T(128)} %constant.51) | copy-start | bytes 28
  82.8 6.3 %copy-start.5 = (s32[2]{0:T(128)S(1)}, s32[2]{0:T(128)}, u32[]{:S(2)}) copy-start(s32[2]{0:T(128)} %constant.54) | copy-start | bytes 28
  82.8 191.9 %all-to-all-start.1 = ((bf16[64,128,512]{2,1,0:T(8,128)(2,1)}), bf16[64,128,512]{2,1,0:T(8,128)(2,1)}, u32[]{:S(2)}, u32[]{:S(2)}) async-start(bf16[64,128,512]{2,1,0:T(8,128)(2,1)} %bitcast.22), calls=%async_computation.1 | async-start | bytes 16777216 | tf_op jit(solution)/shard_map/all_to_all | solution.py:33
  88.7 416.6 %all-reduce.3.cloned.1.call-start = ((), (), s32[]{:S(2)}) async-start(), calls=%async_computation.2 | async-start | bytes 3145728 | tf_op jit(solution)/shard_map/psum | solution.py:66
  281.9 5.7 %copy-start.1 = (f32[8192,512]{1,0:T(8,128)}, f32[8192,512]{1,0:T(8,128)S(1)}, u32[]{:S(2)}) copy-start(f32[8192,512]{1,0:T(8,128)S(1)} %fusion.15) | copy-start | bytes 50331652
  281.9 5.7 %copy-start.2 = (bf16[512,256]{1,0:T(8,128)(2,1)S(1)}, bf16[512,256]{1,0:T(8,128)(2,1)}, u32[]{:S(2)}) copy-start(bf16[512,256]{1,0:T(8,128)(2,1)} %param.11) | copy-start | bytes 786436
  281.9 19.1 %copy-start.4 = (s32[128]{0:T(128)S(1)}, s32[128]{0:T(128)}, u32[]{:S(2)}) copy-start(s32[128]{0:T(128)} %param.9) | copy-start | bytes 1540
Sparse Core Ops, SparseCore 0:
  319.5 185.7 all-reduce.2
